TPU v7x, 32 devices: a whole 2x2x4 slice. The times are simulated.
32 devices in a mesh: dp: 16 (over z, x, core), tensor: 2 (over y).
Axes of the slice: x: 2, y: 2, z: 4, core: 2. Of those that a mesh axis runs over, the one named last changes fastest.
Arguments:
- tokens: bfloat16 [16384, 1024], P('dp'), may hold values from -6 to 6
- segment: int32 [16384], P('dp'), may hold values from 0 to 39, never falling along the last dimension, each value on 1 to 800 neighbouring positions
- norm1_gain: bfloat16 [1024], replicated, may hold values from 0.5 to 1.5
- w_query: bfloat16 [1024, 1024], P(None, 'tensor'), may hold values from -0.1875 to 0.1875
- w_key: bfloat16 [1024, 1024], P(None, 'tensor'), may hold values from -0.1875 to 0.1875
- w_value: bfloat16 [1024, 1728], P(None, 'tensor'), may hold values from -0.1875 to 0.1875
- w_gate: bfloat16 [1024, 1728], P(None, 'tensor'), may hold values from -0.1875 to 0.1875
- group_gain: bfloat16 [1728], P('tensor'), may hold values from 0.5 to 1.5
- group_bias: bfloat16 [1728], P('tensor'), may hold values from -1.5 to 1.5
- w_out: bfloat16 [1728, 1024], P('tensor'), may hold values from -0.15625 to 0.15625
- norm2_gain: bfloat16 [1024], replicated, may hold values from 0.5 to 1.5
- w_mlp_gate: bfloat16 [1024, 1728], P(None, 'tensor'), may hold values from -0.1875 to 0.1875
- w_mlp_up: bfloat16 [1024, 1728], P(None, 'tensor'), may hold values from -0.1875 to 0.1875
- w_mlp_down: bfloat16 [1728, 1024], P('tensor'), may hold values from -0.15625 to 0.15625
- cotangent: bfloat16 [16384, 1024], P('dp'), may hold values from -6 to 6
Outputs:
- output: bfloat16 [16384, 1024], P(('dp', 'tensor'))
- grad_tokens: bfloat16 [16384, 1024], P('dp')
- grad_norm1_gain: float32 [1024], replicated
- grad_w_query: float32 [1024, 1024], P(None, 'tensor')
- grad_w_key: float32 [1024, 1024], P(None, 'tensor')
- grad_w_value: float32 [1024, 1728], P(None, 'tensor')
- grad_w_gate: float32 [1024, 1728], P(None, 'tensor')
- grad_group_gain: float32 [1728], P('tensor')
- grad_group_bias: float32 [1728], P('tensor')
- grad_w_out: float32 [1728, 1024], P('tensor')
- grad_norm2_gain: float32 [1024], replicated
- grad_w_mlp_gate: float32 [1024, 1728], P(None, 'tensor')
- grad_w_mlp_up: float32 [1024, 1728], P(None, 'tensor')
- grad_w_mlp_down: float32 [1728, 1024], P('tensor')
Inputs may be any that keep to these rules, and one draw needn't show every extreme that they name: `segment`: document numbers never fall along the tokens; each document spans 1 to 800 tokens and one spans exactly 800.
All inputs are finite; a program needn't handle non-finite values.
Results may differ from a plain program's by a relative error of at most 0.015.
Values sent between devices are 32-bit elements; how exact they have to be, the bound alone decides.
A program may use at most 256 MiB of HBM per device.

v0:
```python
import functools
import math

import jax
import jax.numpy as jnp
import numpy as np
from jax import lax
from jax.experimental import pallas as pl
from jax.experimental.pallas import tpu as pltpu
from jax.sharding import PartitionSpec as P

KD = 256
VD = 432
LANE = 128
MESH = pl.DeviceIdType.MESH
DELIVER = 4
PIECES = 4
VMEM_LIMIT = 63 * 1024 * 1024


EPSILON = 1e-06
GROUP_EPSILON = 0.25


def ring_place(chip, chips):
    line = chips // 2
    x = chip % 2
    z = chip // 2
    return z + x * (chips - 1 - 2 * z), line


def ring_chip(place, chips):
    line = chips // 2
    x = place // line
    z = place + x * (chips - 1 - 2 * place)
    return z * 2 + x


def bit_partner(index, bit):
    step = 1 << bit
    return index + (1 - 2 * ((index // step) % 2)) * step


BLOCKS = 4
GELU_A = math.sqrt(2.0 / math.pi)
GELU_B = 0.044715


def dot(left, right, left_dim, right_dim):
    return lax.dot_general(
        left, right, (((left_dim,), (right_dim,)), ((), ())), preferred_element_type=jnp.float32
    )


def low(array):
    return array.astype(jnp.bfloat16)


def turn(vectors, cosine, sine):
    half = vectors.shape[1] // 2
    lower, upper = vectors[:, :half], vectors[:, half:]
    return jnp.concatenate([lower * cosine - upper * sine, upper * cosine + lower * sine], axis=1)


def remote(source, target, send, recv, device):
    return pltpu.make_async_remote_copy(
        source, target, send, recv, device_id=device, device_id_type=MESH
    )


def rate_of(head, heads, tensor):
    rates = [math.log1p(-(2.0 ** (-5 - order))) for order in range(2 * heads)]
    return jnp.where(tensor == 0, rates[head], rates[heads + head]).astype(jnp.float32)


def upright(row, size):
    diagonal = lax.broadcasted_iota(jnp.int32, (size, size), 0) == lax.broadcasted_iota(
        jnp.int32, (size, size), 1
    )
    return jnp.sum(jnp.where(diagonal, row, 0.0), axis=1, keepdims=True)


def upright_part(row, start, size):
    shape = (size, row.shape[1])
    chosen = lax.broadcasted_iota(jnp.int32, shape, 0) + start == lax.broadcasted_iota(jnp.int32, shape, 1)
    return jnp.sum(jnp.where(chosen, row, 0.0), axis=1, keepdims=True)


GAIN1, GAIN2, GROUP_GAIN, GROUP_BIAS, SEGMENT = range(5)


def greet(devices):
    barrier = pltpu.get_barrier_semaphore()
    for device in devices:
        pl.semaphore_signal(barrier, inc=1, device_id=device, device_id_type=MESH)
    pl.semaphore_wait(barrier, len(devices))


def mlp_part(gate_w, up_w, down_w, h2, cot, tall, rows):
    a = dot(gate_w[tall, :], h2[rows, :], 1, 1)
    b = dot(up_w[tall, :], h2[rows, :], 1, 1)
    dhidden = dot(down_w[tall, :], cot[rows, :], 1, 1)
    square = a * a
    t = jnp.tanh(GELU_A * a * (1.0 + GELU_B * square))
    gelu = 0.5 * a * (1.0 + t)
    slope = 0.5 * (1.0 + t) + 0.5 * a * (1.0 - t * t) * (GELU_A * (1.0 + 3.0 * GELU_B * square))
    dga = low(dhidden * b * slope)
    dup = low(dhidden * gelu)
    more = dot(dga, gate_w[tall, :], 0, 0) + dot(dup, up_w[tall, :], 0, 0)
    return low(gelu * b), dga, dup, more


def forward_kernel(
    chips,
    x_ref,
    rows_ref,
    cos_ref,
    sin_ref,
    wq_hbm,
    wk_hbm,
    wv_hbm,
    wg_hbm,
    wo_ref,
    mg_ref,
    mu_ref,
    md_ref,
    cot_ref,
    h1_out,
    q_out,
    k_out,
    v_out,
    g_out,
    nh_out,
    rstd_out,
    gated_out,
    mid_out,
    dh_out,
    h2_out,
    hid_out,
    grad_mg_out,
    grad_mu_out,
    grad_md_out,
    gath_out,
    weights,
    others,
    cot,
    h1,
    q,
    k,
    v,
    g,
    nh,
    rstd,
    gated,
    acc,
    gsend,
    grecv,
    h2,
    hid,
    da,
    db,
    mid,
    dh_own,
    sums,
    ggain_ref,
    gbias_ref,
    in_sem,
    save_sem,
    out_sem,
    stage_sem,
    mid_sem,
    dh_sem,
    sum_sem,
    xs_sem,
    xr_sem,
    ys_sem,
    yr_sem,
    gs_sem,
    gr_sem,
    cs_sem,
    cr_sem,
):
    index, tensor = lax.axis_index("dp"), lax.axis_index("tensor")
    core = index % 2
    place, _ = ring_place(index // 2, chips)
    nexts = [
        {"dp": ring_chip((place + 1) % chips, chips) * 2 + core},
        {"dp": ring_chip((place + chips - 1) % chips, chips) * 2 + core},
    ]
    sibling, peer = {"dp": index + 1 - 2 * core}, {"tensor": 1 - tensor}
    heads = q.shape[1]
    units, length = v.shape
    block = length // BLOCKS
    third = units // 3
    f32 = jnp.float32

    for number, source in enumerate((wo_ref, mg_ref, mu_ref, md_ref)):
        pltpu.make_async_copy(source, weights.at[number], in_sem.at[number]).start()
    wv_ref, wg_ref = hid, da
    key_width = wq_hbm.shape[1]
    early = [
        pltpu.make_async_copy(wq_hbm, h2.at[:, pl.ds(0, key_width)], in_sem.at[5]),
        pltpu.make_async_copy(wk_hbm, h2.at[:, pl.ds(key_width, key_width)], in_sem.at[6]),
        pltpu.make_async_copy(wv_hbm, wv_ref, in_sem.at[7]),
        pltpu.make_async_copy(wg_hbm, wg_ref, in_sem.at[8]),
    ]
    for copy in early:
        copy.start()
    pltpu.make_async_copy(cot_ref, cot, in_sem.at[4]).start()
    greet([*nexts, sibling, peer])

    rows_slice = units // 2
    half_slice = rows_slice // 2

    def area(w, where, which, half=None):
        start = which * rows_slice + (0 if half is None else half * half_slice)
        size = rows_slice if half is None else half_slice
        return gath_out.at[
            w,
            pl.ds(pl.multiple_of(start, 8), size),
            pl.ds(pl.multiple_of(where * LANE, LANE), LANE),
        ]

    def slice_spot(w):
        return gsend.at[
            BLOCKS - 1,
            pl.ds((w % 2) * rows_slice, rows_slice),
            pl.ds((w // 2) * LANE, LANE),
        ]

    def y_copy(w):
        return remote(slice_spot(w), area(w, place, core), ys_sem.at[w], yr_sem.at[w], peer)

    def hop(w, d, t):
        where = (place - t + chips) % chips if d == 0 else (place + t) % chips
        part = area(w, where, core, d if t == chips // 2 - 1 else None)
        return remote(part, part, gs_sem.at[w, d, t], gr_sem.at[w, d, t], nexts[d])

    def arrived(w, d, t):
        where = (place - t - 1 + chips) % chips if d == 0 else (place + t + 1) % chips
        part = area(w, where, core, d if t == chips // 2 - 1 else None)
        pltpu.make_async_copy(part, part, gr_sem.at[w, d, t]).wait()
        return where

    def share(w, slot, where, half=None):
        part = area(w, where, core, half)
        remote(part, part, cs_sem.at[w, slot], cr_sem.at[w, slot], sibling).start()

    steps = chips // 2

    def begin(w):
        y_copy(w).wait_recv()
        for d in range(2):
            hop(w, d, 0).start()
        share(w, 0, place)

    def pump(w, t):
        for d in range(2):
            where = arrived(w, d, t)
            if t < steps - 1:
                hop(w, d, t + 1).start()
            share(w, 1 + 2 * t + d, where, d if t == steps - 1 else None)

    for number in range(4):
        pltpu.make_async_copy(wo_ref, weights.at[number], in_sem.at[number]).wait()
        slice_spot(number)[...] = weights[
            number,
            pl.ds(pl.multiple_of(core * rows_slice, 16), rows_slice),
            pl.ds(pl.multiple_of(place * LANE, LANE), LANE),
        ].astype(f32)
        y_copy(number).start()

    def exchange(i):
        return remote(gsend.at[i], grecv.at[i], xs_sem.at[i], xr_sem.at[i], peer)

    ahead = lax.broadcasted_iota(jnp.int32, (block, block), 0) - lax.broadcasted_iota(
        jnp.int32, (block, block), 1
    )

    def saves(i):
        slot = i % 2
        rows = pl.ds(pl.multiple_of(i * block, block), block)
        pairs = (
            (h1.at[slot], h1_out.at[rows, :]),
            (q.at[slot], q_out.at[:, rows, :]),
            (g.at[slot], g_out.at[:, rows]),
            (nh.at[slot], nh_out.at[:, rows]),
        )
        return [
            pltpu.make_async_copy(source, target, save_sem.at[number, slot])
            for number, (source, target) in enumerate(pairs)
        ]

    def attention(i, carry):
        rows = pl.ds(pl.multiple_of(i * block, block), block)
        slot = i % 2

        @pl.when(i >= 2)
        def _():
            for copy in saves(i - 2):
                copy.wait()

        xb = x_ref[rows, :].astype(f32)
        r1 = lax.rsqrt(jnp.mean(xb * xb, axis=1, keepdims=True) + EPSILON)
        h1[slot] = low(xb * r1 * rows_ref[GAIN1 : GAIN1 + 1, :])
        cosine, sine = cos_ref[rows, :], sin_ref[rows, :]
        for head in range(heads):
            wide = slice(head * KD, (head + 1) * KD)
            q[slot, head] = low(turn(dot(h1[slot], h2[:, wide], 1, 0), cosine, sine))
            wide = slice(key_width + head * KD, key_width + (head + 1) * KD)
            k[head, rows, :] = low(turn(dot(h1[slot], h2[:, wide], 1, 0), cosine, sine) * KD ** (-0.5))
        v[:, rows] = low(dot(wv_ref[...], h1[slot], 1, 1))

        @pl.when(i == BLOCKS - 1)
        def _():
            for w in range(4):
                y_copy(w).wait_send()

        segc = upright(rows_ref[SEGMENT : SEGMENT + 1, rows], block)
        for head in range(heads):
            tall = slice(head * VD, (head + 1) * VD)
            rate = rate_of(head, heads, tensor)
            acc[...] = jnp.zeros_like(acc)

            def tile(m, carry):
                cols = pl.ds(pl.multiple_of(m * block, block), block)
                s = dot(q[slot, head], k[head, cols, :], 1, 1)
                gap = ahead + (i - m) * block
                seen = (segc == rows_ref[SEGMENT : SEGMENT + 1, cols]) & (gap >= 0)
                s = jnp.where(seen, s * jnp.exp(gap.astype(f32) * rate), 0.0)
                acc[...] += dot(v[tall, cols], low(s), 1, 1)
                return carry

            lax.fori_loop(0, i + 1, tile, 0)
            ret = acc[...]
            centred = ret - jnp.mean(ret, axis=0, keepdims=True)
            scale = lax.rsqrt(jnp.mean(centred * centred, axis=0, keepdims=True) + GROUP_EPSILON)
            nhat = centred * scale
            nh[slot, tall, :] = low(nhat)
            rstd[head : head + 1, rows] = scale
            gate = dot(wg_ref[tall, :], h1[slot], 1, 1)
            g[slot, tall, :] = low(gate)
            gn = nhat * ggain_ref[tall, :] + gbias_ref[tall, :]
            out = low(gate / (1.0 + jnp.exp(-gate)) * gn)
            gated[tall, rows] = out
            gsend[i, tall, :] = out.astype(f32)
        exchange(i).start()
        for copy in saves(i):
            copy.start()

        @pl.when(i == 0)
        def _():
            begin(0)

        @pl.when(i == 1)
        def _():
            pump(0, 0)
            for w in range(1, 4):
                begin(w)

        @pl.when(i == 2)
        def _():
            pump(0, 1)

        return carry

    rstd[...] = jnp.zeros_like(rstd)
    for n in range(3):
        where = slice(n * third, (n + 1) * third)
        ggain_ref[where, :] = upright_part(rows_ref[GROUP_GAIN : GROUP_GAIN + 1, :], n * third, third)
        gbias_ref[where, :] = upright_part(rows_ref[GROUP_BIAS : GROUP_BIAS + 1, :], n * third, third)
    for copy in early:
        copy.wait()
    lax.fori_loop(0, BLOCKS, attention, 0)
    for i in range(BLOCKS - 2, BLOCKS):
        for copy in saves(i):
            copy.wait()
    saved = [(k, k_out), (v, v_out), (rstd, rstd_out), (gated, gated_out)]
    for number, (source, target) in enumerate(saved):
        pltpu.make_async_copy(source, target, out_sem.at[number]).start()

    def cast_ready(w):
        for slot in range(1 + 2 * steps):
            t = (slot - 1) // 2
            d = (slot - 1) % 2
            if slot == 0:
                where = place
            else:
                where = (place - t - 1 + chips) % chips if d == 0 else (place + t + 1) % chips
            part = area(w, where, 1 - core, d if slot > 0 and t == steps - 1 else None)
            pltpu.make_async_copy(part, part, cr_sem.at[w, slot]).wait()

    def stage(number):
        return sums.at[0, pl.ds((number % 2) * third, third), :]

    def cast_in(ws):
        pieces = [(w, n) for w in ws for n in range(3)]

        def piece(number):
            w, n = pieces[number]
            return pltpu.make_async_copy(
                gath_out.at[w, pl.ds(n * third, third), :], stage(number), stage_sem.at[number % 2]
            )

        cast_ready(ws[0])
        piece(0).start()
        for number, (w, n) in enumerate(pieces):
            if number + 1 < len(pieces):
                if pieces[number + 1][1] == 0:
                    cast_ready(pieces[number + 1][0])
                piece(number + 1).start()
            piece(number).wait()
            others[n * third : (n + 1) * third, :] = low(stage(number)[...])

    pump(0, 2)
    pump(0, 3)
    cast_in([0])
    pltpu.make_async_copy(cot_ref, cot, in_sem.at[4]).wait()
    part = units // 2

    def mid_copy(i):
        rows = pl.ds(pl.multiple_of(i * block, block), block)
        return pltpu.make_async_copy(mid.at[i % 2], mid_out.at[rows, :], mid_sem.at[i % 2])

    def dh_copy(i):
        rows = pl.ds(pl.multiple_of(i * block, block), block)
        return pltpu.make_async_copy(dh_own.at[i % 2], dh_out.at[rows, :], dh_sem.at[i % 2])

    def own_half(i):
        rows = pl.ds(pl.multiple_of(i * block, block), block)
        slot = i % 2

        @pl.when(i >= 2)
        def _():
            mid_copy(i - 2).wait()
            dh_copy(i - 2).wait()

        exchange(i).wait_recv()
        mid[slot] = x_ref[rows, :].astype(f32) + (
            dot(gated[:, rows], weights[0], 0, 0) + dot(low(grecv[i]), others[...], 0, 0)
        )
        mid_copy(i).start()
        r2 = lax.rsqrt(jnp.mean(mid[slot] * mid[slot], axis=1, keepdims=True) + EPSILON)
        h2[rows, :] = low(mid[slot] * r2 * rows_ref[GAIN2 : GAIN2 + 1, :])
        for f in range(2):
            tall = slice(f * part, (f + 1) * part)
            hid[tall, rows], da[tall, rows], db[tall, rows], more = mlp_part(
                weights.at[1], weights.at[2], weights.at[3], h2, cot, tall, rows
            )
            dh_own[slot] = more if f == 0 else dh_own[slot] + more
        dh_copy(i).start()

    def first_pass(i, carry):
        for t in range(3):

            @pl.when(i == t)
            def _():
                for w in range(1, 4):
                    pump(w, t)

        own_half(i)
        return carry

    products = ((da, h2, grad_mg_out), (db, h2, grad_mu_out), (hid, cot, grad_md_out))
    before = (BLOCKS - 1) * block
    lax.fori_loop(0, BLOCKS - 1, first_pass, 0)
    for w in range(1, 4):
        pump(w, 3)
    for number, (source, right, _) in enumerate(products):
        for n in range(3):
            where = slice(n * third, (n + 1) * third)
            sums[number, where, :] = dot(source[where, 0:before], right[0:before, :], 1, 0)
    own_half(BLOCKS - 1)
    late = [
        pltpu.make_async_copy(h2, h2_out, out_sem.at[4]),
        pltpu.make_async_copy(hid, hid_out, out_sem.at[5]),
    ]
    for copy in late:
        copy.start()
    for number, (source, right, target) in enumerate(products):
        for n in range(3):
            where = slice(n * third, (n + 1) * third)
            sums[number, where, :] += dot(source[where, before:length], right[before:length, :], 1, 0)
            late.append(
                pltpu.make_async_copy(
                    sums.at[number, pl.ds(n * third, third), :],
                    target.at[pl.ds(n * third, third), :],
                    sum_sem.at[number, n],
                )
            )
            late[-1].start()
    for copy in late:
        copy.wait()
    for w in range(1, 4):
        cast_ready(w)
    for i in range(BLOCKS - 2, BLOCKS):
        mid_copy(i).wait()
        dh_copy(i).wait()
    for number, (source, target) in enumerate(saved):
        pltpu.make_async_copy(source, target, out_sem.at[number]).wait()
    for w in range(4):
        for t in range(steps):
            for d in range(2):
                hop(w, d, t).wait_send()
        for slot in range(1 + 2 * steps):
            last = slot > 0 and (slot - 1) // 2 == steps - 1
            part_ref = area(w, place, core, 0 if last else None)
            pltpu.make_async_copy(part_ref, part_ref, cs_sem.at[w, slot]).wait()
    for i in range(BLOCKS):
        exchange(i).wait_send()


def forward(tokens, vectors, tables, ws, cotangent):
    chips = lax.axis_size("dp") // 2
    length, depth = tokens.shape
    wq, wk, wv, wg, wo, mg, mu, md = ws
    units = wv.shape[0]
    heads = wq.shape[1] // KD
    block = length // BLOCKS
    f32, bf16 = jnp.float32, jnp.bfloat16
    vmem = pl.BlockSpec(memory_space=pltpu.VMEM)
    hbm = pl.BlockSpec(memory_space=pl.ANY)
    dma = lambda *shape: pltpu.SemaphoreType.DMA(shape)
    shape = jax.ShapeDtypeStruct
    tall = (units, length)
    steps = chips // 2
    outs = [
        (shape((length, depth), bf16), hbm),
        (shape((heads, length, KD), bf16), hbm),
        (shape((heads, length, KD), bf16), hbm),
        (shape(tall, bf16), hbm),
        (shape(tall, bf16), hbm),
        (shape(tall, bf16), hbm),
        (shape((8, length), f32), hbm),
        (shape(tall, bf16), hbm),
        (shape((length, depth), f32), hbm),
        (shape((length, depth), f32), hbm),
        (shape((length, depth), bf16), hbm),
        (shape(tall, bf16), hbm),
        (shape((units, depth), f32), hbm),
        (shape((units, depth), f32), hbm),
        (shape((units, depth), f32), hbm),
        (shape((4, units, depth), f32), hbm),
    ]
    scratch = [
        pltpu.VMEM((4, units, depth), bf16),
        pltpu.VMEM((units, depth), bf16),
        pltpu.VMEM((length, depth), bf16),
        pltpu.VMEM((2, block, depth), bf16),
        pltpu.VMEM((2, heads, block, KD), bf16),
        pltpu.VMEM((heads, length, KD), bf16),
        pltpu.VMEM(tall, bf16),
        pltpu.VMEM((2, units, block), bf16),
        pltpu.VMEM((2, units, block), bf16),
        pltpu.VMEM((8, length), f32),
        pltpu.VMEM(tall, bf16),
        pltpu.VMEM((VD, block), f32),
        pltpu.VMEM((BLOCKS, units, block), f32),
        pltpu.VMEM((BLOCKS, units, block), f32),
        pltpu.VMEM((length, depth), bf16),
        pltpu.VMEM(tall, bf16),
        pltpu.VMEM(tall, bf16),
        pltpu.VMEM(tall, bf16),
        pltpu.VMEM((2, block, depth), f32),
        pltpu.VMEM((2, block, depth), f32),
        pltpu.VMEM((3, units, depth), f32),
        pltpu.VMEM((units, 1), f32),
        pltpu.VMEM((units, 1), f32),
        dma(9),
        dma(4, 2),
        dma(6),
        dma(2),
        dma(2),
        dma(2),
        dma(3, 3),
        dma(BLOCKS),
        dma(BLOCKS),
        dma(4),
        dma(4),
        dma(4, 2, steps),
        dma(4, 2, steps),
        dma(4, 1 + 2 * steps),
        dma(4, 1 + 2 * steps),
    ]
    return pl.pallas_call(
        functools.partial(forward_kernel, chips),
        out_shape=tuple(o for o, _ in outs),
        in_specs=[vmem] * 4 + [hbm] * 9,
        out_specs=tuple(s for _, s in outs),
        scratch_shapes=scratch,
        compiler_params=pltpu.CompilerParams(
            collective_id=1, has_side_effects=True, vmem_limit_bytes=VMEM_LIMIT
        ),
        cost_estimate=pl.CostEstimate(
            flops=40 * length * depth * units, bytes_accessed=80 * length * depth, transcendentals=0
        ),
    )(tokens, vectors, *tables, wq, wk, wv, wg, wo, mg, mu, md, cotangent)


def make_tables(length):
    half = KD // 2
    frequency = np.exp(-np.log(10000.0) * np.arange(half) / half)
    angles = np.arange(length)[:, None] * frequency[None, :]
    return jnp.asarray(np.cos(angles), jnp.float32), jnp.asarray(np.sin(angles), jnp.float32)


def pack_rows(arrays, width):
    rows = [jnp.pad(a.astype(jnp.float32), (0, width - a.shape[0])) for a in arrays]
    return jnp.pad(jnp.stack(rows), ((0, 8 - len(rows)), (0, 0)))


class Ring:
    def __init__(self, chips, quarters, own, sib, rcv, own_sem, sbs_sem, sbr_sem, rss_sem, rsr_sem):
        self.chips, self.quarters = chips, quarters
        self.index, self.tensor = lax.axis_index("dp"), lax.axis_index("tensor")
        self.core = self.index % 2
        place, _ = ring_place(self.index // 2, chips)
        self.place = place
        self.nexts = [
            {"dp": ring_chip((place + 1) % chips, chips) * 2 + self.core},
            {"dp": ring_chip((place + chips - 1) % chips, chips) * 2 + self.core},
        ]
        self.virtual = [place, (chips - place) % chips]
        self.sibling = {"dp": self.index + 1 - 2 * self.core}
        self.peer = {"tensor": 1 - self.tensor}
        self.offsets = [sum(quarters[:i]) for i in range(len(quarters))]
        self.own, self.sib, self.rcv = own, sib, rcv
        self.own_sem, self.sbs_sem, self.sbr_sem = own_sem, sbs_sem, sbr_sem
        self.rss_sem, self.rsr_sem = rss_sem, rsr_sem
        self.tokens = [(d, a) for a in range(len(quarters)) for d in range(2)]

    def window(self, which, d, chunk, rows):
        return (
            pl.ds(pl.multiple_of((which * 2 + d) * rows, 8), rows),
            pl.ds(pl.multiple_of(chunk * LANE, LANE), LANE),
        )

    def packed(self, a):
        return pl.ds(self.offsets[a], self.quarters[a])

    def chunk_at(self, d, order):
        return (self.virtual[d] + 2 * self.chips - 1 - order) % self.chips

    def quarter(self, which, d, a):
        rows = self.quarters[a]
        return pl.ds(pl.multiple_of((which * 2 + d) * rows, 8), rows)

    def own_copy(self, grads, d, a):
        return pltpu.make_async_copy(
            grads[a].at[self.quarter(self.core, d, a), :],
            self.own.at[d, self.packed(a), :],
            self.own_sem.at[d, a],
        )

    def sib_copy(self, grads, d, a):
        return remote(
            grads[a].at[self.quarter(1 - self.core, d, a), :],
            self.sib.at[d, self.packed(a), :],
            self.sbs_sem.at[d, a],
            self.sbr_sem.at[d, a],
            self.sibling,
        )

    def load(self, grads):
        for d, a in self.tokens:
            self.own_copy(grads, d, a).start()
            self.sib_copy(grads, d, a).start()

    def columns(self, d, order):
        return pl.ds(pl.multiple_of(self.chunk_at(d, order) * LANE, LANE), LANE)

    def chunk(self, d, a, order):
        return self.own.at[d, self.packed(a), self.columns(d, order)]

    def rs_copy(self, d, a, step):
        return remote(
            self.chunk(d, a, step),
            self.rcv.at[d, step, self.packed(a), :],
            self.rss_sem.at[d, a, step],
            self.rsr_sem.at[d, a, step],
            self.nexts[d],
        )

    def total(self, grads, d, a, step, first=False):
        if first:
            self.own_copy(grads, d, a).wait()
            self.sib_copy(grads, d, a).wait_recv()
        part, where = self.packed(a), self.columns(d, step)
        value = self.own[d, part, where] + self.sib[d, part, where]
        if not first:
            self.rs_copy(d, a, step - 1).wait_recv()
            value = value + self.rcv[d, step - 1, part, :]
        self.own[d, part, where] = value

    def drain_ring(self):
        def ring_step(step, carry):
            for d, a in self.tokens:
                self.rs_copy(d, a, step).wait_send()
            return carry

        lax.fori_loop(0, self.chips - 1, ring_step, 0)

    def drain_pair(self, grads):
        for d, a in self.tokens:
            self.sib_copy(grads, d, a).wait_send()


class Spread:
    def __init__(self, ring, quarters, outs, buffer, ags_sem, agr_sem, cgs_sem, cgr_sem, loc_sem):
        self.ring, self.quarters, self.outs, self.buffer = ring, quarters, outs, buffer
        self.ags_sem, self.agr_sem, self.cgs_sem, self.cgr_sem, self.loc_sem = (
            ags_sem, agr_sem, cgs_sem, cgr_sem, loc_sem,
        )
        self.offsets = [sum(quarters[:i]) for i in range(len(quarters))]
        self.tokens = [(d, a) for a in range(len(quarters)) for d in range(2)]

    def packed(self, a):
        return pl.ds(self.offsets[a], self.quarters[a])

    def part(self, which, d, a, step):
        ring = self.ring
        chunk = (ring.virtual[d] + 2 * ring.chips - step) % ring.chips
        return self.outs[a].at[ring.window(which, d, chunk, self.quarters[a])]

    def slot(self, d, a, step):
        return self.buffer.at[d, step, self.packed(a), :]

    def ring_copy(self, d, a, step, source=None):
        return remote(
            self.slot(d, a, step - 1) if source is None else source,
            self.slot(d, a, step),
            self.ags_sem.at[d, a, step],
            self.agr_sem.at[d, a, step],
            self.ring.nexts[d],
        )

    def pair_copy(self, d, a, step, source=None):
        return remote(
            self.slot(d, a, step - 1) if source is None else source,
            self.part(self.ring.core, d, a, step),
            self.cgs_sem.at[d, a, step],
            self.cgr_sem.at[d, a, step],
            self.ring.sibling,
        )

    def local_copy(self, d, a, step, source=None):
        return pltpu.make_async_copy(
            self.slot(d, a, step - 1) if source is None else source,
            self.part(self.ring.core, d, a, step),
            self.loc_sem.at[d, a, step],
        )

    def place(self, d, a, step, source=None):
        self.pair_copy(d, a, step, source).start()
        self.local_copy(d, a, step, source).start()

    def arrived(self, d, a, step):
        part = self.slot(d, a, step)
        pltpu.make_async_copy(part, part, self.agr_sem.at[d, a, step]).wait()

    def finish(self, step):
        for d, a in self.tokens:
            self.arrived(d, a, step)
            self.place(d, a, step + 1)

    def drain_ring(self):
        def ring_step(step, carry):
            for d, a in self.tokens:
                part = self.slot(d, a, step)
                pltpu.make_async_copy(part, part, self.ags_sem.at[d, a, step]).wait()
            return carry

        lax.fori_loop(0, self.ring.chips - 1, ring_step, 0)

    def drain(self):
        def pair_step(step, carry):
            for d, a in self.tokens:
                part = self.part(self.ring.core, d, a, step)
                pltpu.make_async_copy(part, part, self.cgs_sem.at[d, a, step]).wait()
                pltpu.make_async_copy(part, part, self.cgr_sem.at[d, a, step]).wait()
                pltpu.make_async_copy(part, part, self.loc_sem.at[d, a, step]).wait()
            return carry

        lax.fori_loop(0, self.ring.chips, pair_step, 0)


def backward_kernel(
    chips,
    quarters,
    x_hbm,
    rows_ref,
    cos_ref,
    sin_ref,
    cot_hbm,
    h2_hbm,
    hid_hbm,
    md_hbm,
    mid_hbm,
    dh_hbm,
    gath_hbm,
    wo_hbm,
    g_hbm,
    nh_hbm,
    rstd_hbm,
    q_hbm,
    k_hbm,
    v_hbm,
    wq_hbm,
    wk_hbm,
    wv_hbm,
    wg_hbm,
    h1_hbm,
    gated_hbm,
    grad_mg,
    grad_mu,
    grad_md,
    dmid_out,
    output_out,
    grad_mg_out,
    grad_mu_out,
    grad_md_out,
    part_out,
    grad_qk_out,
    grad_v_out,
    grad_g_out,
    grad_out_out,
    small_out,
    x,
    branch,
    wo,
    g,
    nh,
    rstd,
    q,
    k,
    v,
    wq,
    wk,
    wv,
    wg,
    h1,
    gated,
    acc_gain,
    acc_bias,
    dk,
    dv,
    dq,
    stage,
    fin,
    finished,
    own,
    sib,
    rcv,
    buffer,
    ggain_ref,
    gbias_ref,
    segc_ref,
    in_sem,
    stage_sem,
    column_sem,
    fin_sem,
    dmid_sem,
    output_sem,
    own_sem,
    sbs_sem,
    sbr_sem,
    rss_sem,
    rsr_sem,
    *spread_sems,
):
    ring = Ring(chips, quarters, own, sib, rcv, own_sem, sbs_sem, sbr_sem, rss_sem, rsr_sem)
    grads = (grad_mg, grad_mu, grad_md)
    spread = Spread(ring, quarters, (grad_mg_out, grad_mu_out, grad_md_out), buffer, *spread_sems)
    f32 = jnp.float32
    heads = q.shape[0]
    length = h1.shape[0]
    units = v.shape[0]
    block = length // BLOCKS
    third = units // 3
    cot, h2, hid, md = x, h1, gated, v
    mg_o, mu_o, md_o = wv, wg, wo
    pairs = [
        (cot_hbm, cot), (h2_hbm, h2), (hid_hbm, hid), (md_hbm, md),
        (g_hbm, g), (nh_hbm, nh), (rstd_hbm, rstd), (q_hbm, q), (k_hbm, k), (wq_hbm, wq), (wk_hbm, wk),
        (wo_hbm, wo), (v_hbm, v), (wv_hbm, wv), (wg_hbm, wg), (x_hbm, x), (h1_hbm, h1), (gated_hbm, gated),
    ]
    copies = [pltpu.make_async_copy(a, b, in_sem.at[n]) for n, (a, b) in enumerate(pairs)]
    greet([*ring.nexts, ring.sibling])
    ring.load(grads)

    cast_list = [(w, target, n) for w, target in ((1, mg_o), (2, mu_o), (3, md_o)) for n in range(3)]

    def cast_copy(number):
        w, _, n = cast_list[number]
        return pltpu.make_async_copy(
            gath_hbm.at[w, pl.ds(n * third, third), :], stage.at[number % 2], stage_sem.at[number % 2]
        )

    cast_copy(0).start()
    for copy in copies[:4]:
        copy.start()
    for copy in copies[4:11]:
        copy.start()
    acc_gain[...] = jnp.zeros_like(acc_gain)
    acc_bias[...] = jnp.zeros_like(acc_bias)
    small_out[...] = jnp.zeros_like(small_out)
    for n in range(3):
        where = slice(n * third, (n + 1) * third)
        ggain_ref[where, :] = upright_part(rows_ref[GROUP_GAIN : GROUP_GAIN + 1, :], n * third, third)
        gbias_ref[where, :] = upright_part(rows_ref[GROUP_BIAS : GROUP_BIAS + 1, :], n * third, third)
    for n in range(BLOCKS):
        where = slice(n * block, (n + 1) * block)
        segc_ref[where, :] = upright(rows_ref[SEGMENT : SEGMENT + 1, where], block)
    plan = [(step, a) for step in range(2 * chips - 1) for a in range(len(quarters))]

    def pump(count=1):
        for _ in range(min(count, len(plan))):
            step, a = plan.pop(0)
            for d in range(2):
                if step < chips:
                    ring.total(grads, d, a, step, step == 0)
                if step < chips - 1:
                    ring.rs_copy(d, a, step).start()
                    continue
                turn_step = step - (chips - 1)
                source = ring.chunk(d, a, chips - 1) if turn_step == 0 else None
                if turn_step > 0:
                    spread.arrived(d, a, turn_step - 1)
                if turn_step < chips - 1:
                    spread.ring_copy(d, a, turn_step, source).start()
                spread.place(d, a, turn_step, source)

    fin_rows = [pl.ds(i * block, block) for i in range(BLOCKS)]

    def fin_copy(i, which):
        source = (mid_hbm, dh_hbm)[which]
        return pltpu.make_async_copy(source.at[fin_rows[i], :], fin.at[which], fin_sem.at[which])

    for which in range(2):
        fin_copy(0, which).start()
    for number, (_, target, n) in enumerate(cast_list):
        if number + 1 < len(cast_list):
            cast_copy(number + 1).start()
        cast_copy(number).wait()
        target[n * third : (n + 1) * third, :] = low(stage[number % 2])
        if number % 2 == 0:
            pump()
    for copy in copies[:4]:
        copy.wait()
    dh_oth, out_sum = stage.at[0, pl.ds(0, block), :], stage.at[1, pl.ds(0, block), :]
    half_units = units // 2

    def output_copy(i):
        spot = pl.ds((i % (BLOCKS // 2)) * block, block)
        return pltpu.make_async_copy(finished, output_out.at[spot, :], output_sem)

    def dmid_copy(i):
        return pltpu.make_async_copy(fin.at[1], dmid_out.at[fin_rows[i], :], dmid_sem)

    gain2 = rows_ref[GAIN2 : GAIN2 + 1, :]
    for i in range(BLOCKS):
        rows = fin_rows[i]
        for which in range(2):
            fin_copy(i, which).wait()
        mine = ring.tensor == i // (BLOCKS // 2)
        for f in range(2):
            tall = slice(f * half_units, (f + 1) * half_units)
            hidden, _, _, more = mlp_part(mg_o, mu_o, md_o, h2, cot, tall, rows)
            dh_oth[...] = more if f == 0 else dh_oth[...] + more

            @pl.when(mine)
            def _():
                lift = dot(hidden, md_o[tall, :], 0, 0) + dot(hid[tall, rows], md[tall, :], 0, 0)
                out_sum[...] = lift if f == 0 else out_sum[...] + lift

            pump()

        @pl.when(mine)
        def _():
            if i % (BLOCKS // 2):
                output_copy(i - 1).wait()
            finished[...] = low(fin[0] + out_sum[...])
            output_copy(i).start()

        mid = fin[0]
        r2 = lax.rsqrt(jnp.mean(mid * mid, axis=1, keepdims=True) + EPSILON)
        dh2 = fin[1] + dh_oth[...]
        e = dh2 * gain2
        inner = jnp.mean(e * mid, axis=1, keepdims=True)
        small_out[1:2, :] += jnp.sum(dh2 * mid * r2, axis=0, keepdims=True)
        result = cot[rows, :].astype(f32) + r2 * e - mid * (r2 * r2 * r2 * inner)
        fin[1] = result
        branch[rows, :] = low(result)
        dmid_copy(i).start()
        if i < BLOCKS - 1:
            fin_copy(i + 1, 0).start()
            dmid_copy(i).wait()
            fin_copy(i + 1, 1).start()
        pump()
    for copy in copies[11:]:
        copy.start()
    for copy in copies[4:7]:
        copy.wait()
    copies[11].wait()

    def fold(values):
        return values[:, :LANE] + values[:, LANE:]

    def gate_block(i):
        rows = pl.ds(i * block, block)
        for head in range(heads):
            tall = slice(head * VD, (head + 1) * VD)
            up = dot(wo[tall, :], branch[rows, :], 1, 1)
            gate = g[tall, rows].astype(f32)
            nhat = nh[tall, rows].astype(f32)
            sigmoid = 1.0 / (1.0 + jnp.exp(-gate))
            silu = gate * sigmoid
            dgn = up * silu
            acc_gain[tall, :] += fold(dgn * nhat)
            acc_bias[tall, :] += fold(dgn)
            gain = ggain_ref[tall, :]
            f = dgn * gain
            mean = jnp.mean(f, axis=0, keepdims=True)
            inner = jnp.mean(f * nhat, axis=0, keepdims=True)
            nh[tall, rows] = low((f - mean - nhat * inner) * rstd[head : head + 1, rows])
            gn = nhat * gain + gbias_ref[tall, :]
            g[tall, rows] = low(up * gn * (sigmoid + silu * (1.0 - sigmoid)))

    for i in range(BLOCKS):
        gate_block(i)
        pump()
    for copy in (copies[7], copies[8], copies[12]):
        copy.wait()

    ahead = lax.broadcasted_iota(jnp.int32, (block, block), 0) - lax.broadcasted_iota(
        jnp.int32, (block, block), 1
    )

    def key_block(head, m):
        tall = slice(head * VD, (head + 1) * VD)
        cols = pl.ds(m * block, block)
        rate = rate_of(head, heads, ring.tensor)
        dk[...] = jnp.zeros_like(dk)
        dv[...] = jnp.zeros_like(dv)

        def tile(i, carry):
            rows = pl.ds(pl.multiple_of(i * block, block), block)
            gap = ahead + (i - m) * block
            seen = (segc_ref[rows, :] == rows_ref[SEGMENT : SEGMENT + 1, cols]) & (gap >= 0)
            decay = jnp.where(seen, jnp.exp(gap.astype(f32) * rate), 0.0)
            scores = low(dot(q[head, rows, :], k[head, cols, :], 1, 1) * decay)
            draw = low(dot(nh[tall, rows], v[tall, cols], 0, 0) * decay)
            dv[...] += dot(nh[tall, rows], scores, 1, 0)
            dk[...] += dot(draw, q[head, rows, :], 0, 0)
            more = dot(draw, k[head, cols, :], 1, 0)
            if m == 0:
                dq[rows, :] = more
            else:
                dq[rows, :] += more
            return carry

        if m == 0:
            lax.fori_loop(0, BLOCKS // 2, tile, 0)
            pump()
            lax.fori_loop(BLOCKS // 2, BLOCKS, tile, 0)
        else:
            lax.fori_loop(m, BLOCKS, tile, 0)
        v[tall, cols] = low(dv[...])
        k[head, cols, :] = low(turn(dk[...], cos_ref[cols, :], -sin_ref[cols, :]) * KD ** (-0.5))

    for head in range(heads):
        for m in range(BLOCKS):
            key_block(head, m)
            if m == BLOCKS - 1:
                q[head] = low(turn(dq[...], cos_ref[...], -sin_ref[...]))
            pump()

    for copy in (*copies[9:11], *copies[13:]):
        copy.wait()
    column = dq

    def stage_wait(slot):
        pltpu.make_async_copy(stage.at[slot], stage.at[slot], stage_sem.at[slot]).wait()

    key_parts = [(q, wq), (k, wk)]
    for i in range(BLOCKS):
        slot = i % 2
        rows = pl.ds(i * block, block)
        if i >= 2:
            stage_wait(slot)
        total = None
        for values, weights in key_parts:
            for head in range(heads):
                wide = slice(head * KD, (head + 1) * KD)
                more = dot(values[head, rows, :], weights[:, wide], 1, 1)
                total = more if total is None else total + more
        stage[slot, 0:block, :] = total
        stage[slot, 0:block, :] += dot(v[:, rows], wv[...], 0, 0)
        stage[slot, 0:block, :] += dot(g[:, rows], wg[...], 0, 0)
        xb = x[rows, :].astype(f32)
        r1 = lax.rsqrt(jnp.mean(xb * xb, axis=1, keepdims=True) + EPSILON)
        small_out[0:1, :] += jnp.sum(stage[slot, 0:block, :] * (xb * r1), axis=0, keepdims=True)
        pltpu.make_async_copy(stage.at[slot], part_out.at[i], stage_sem.at[slot]).start()
        pump()

    count = BLOCKS
    for source, right, target in ((v, h1, grad_v_out), (g, h1, grad_g_out), (gated, branch, grad_out_out)):
        for n in range(3):
            where = pl.ds(n * third, third)
            slot = count % 2
            stage_wait(slot)
            stage[slot] = dot(source[where, :], right[...], 1, 0)
            pltpu.make_async_copy(stage.at[slot], target.at[where, :], stage_sem.at[slot]).start()
            count += 1
            pump()

    for number, (values, head) in enumerate([(q, 0), (q, 1), (k, 0), (k, 1)][: 2 * heads]):
        if number:
            pltpu.make_async_copy(column, column, column_sem).wait()
        column[...] = dot(h1[...], values[head], 0, 0)
        pltpu.make_async_copy(column, grad_qk_out.at[:, pl.ds(number * KD, KD)], column_sem).start()
        pump()
    pump(len(plan))

    ones = jnp.ones((8, LANE), jnp.bfloat16)

    def row_of(acc):
        whole = acc[...]
        high = low(whole)
        return dot(ones, high, 1, 1) + dot(ones, low(whole - high.astype(f32)), 1, 1)

    small_out[2:3, 0:units] = row_of(acc_gain)[0:1, :]
    small_out[3:4, 0:units] = row_of(acc_bias)[0:1, :]

    ring.drain_ring()
    ring.drain_pair(grads)
    spread.drain_ring()
    spread.drain()
    dmid_copy(BLOCKS - 1).wait()
    output_copy(BLOCKS - 1).wait()
    for slot in range(2):
        stage_wait(slot)
    pltpu.make_async_copy(column, column, column_sem).wait()


def backward(tokens, vectors, tables, cotangent, mlp, saved, ws, mlp_grads):
    chips = lax.axis_size("dp") // 2
    length, depth = tokens.shape
    wq, wk, wv, wg, wo, md = ws
    h1, q, k, v, g, nh, rstd, gated = saved
    mid, dh, h2, hid, gathered = mlp
    units = wv.shape[0]
    heads = q.shape[0]
    block = length // BLOCKS
    quarters = tuple(a.shape[0] // 4 for a in mlp_grads)
    rows = sum(quarters)
    count = len(quarters)
    f32, bf16 = jnp.float32, jnp.bfloat16
    vmem = pl.BlockSpec(memory_space=pltpu.VMEM)
    hbm = pl.BlockSpec(memory_space=pl.ANY)
    dma = lambda *shape: pltpu.SemaphoreType.DMA(shape)
    shape = jax.ShapeDtypeStruct
    tall = (units, length)
    stage_rows = max(block, units // 3)
    outs = [
        (shape((length, depth), f32), hbm),
        (shape((length // 2, depth), bf16), hbm),
        (shape((units, depth), f32), hbm),
        (shape((units, depth), f32), hbm),
        (shape((units, depth), f32), hbm),
        (shape((BLOCKS, stage_rows, depth), f32), hbm),
        (shape((depth, 2 * heads * KD), f32), hbm),
        (shape((units, depth), f32), hbm),
        (shape((units, depth), f32), hbm),
        (shape((units, depth), f32), hbm),
        (shape((8, depth), f32), vmem),
    ]
    scratch = [
        pltpu.VMEM((length, depth), bf16),
        pltpu.VMEM((length, depth), bf16),
        pltpu.VMEM((units, depth), bf16),
        pltpu.VMEM(tall, bf16),
        pltpu.VMEM(tall, bf16),
        pltpu.VMEM((8, length), f32),
        pltpu.VMEM((heads, length, KD), bf16),
        pltpu.VMEM((heads, length, KD), bf16),
        pltpu.VMEM(tall, bf16),
        pltpu.VMEM((depth, heads * KD), bf16),
        pltpu.VMEM((depth, heads * KD), bf16),
        pltpu.VMEM((units, depth), bf16),
        pltpu.VMEM((units, depth), bf16),
        pltpu.VMEM((length, depth), bf16),
        pltpu.VMEM(tall, bf16),
        pltpu.VMEM((units, LANE), f32),
        pltpu.VMEM((units, LANE), f32),
        pltpu.VMEM((block, KD), f32),
        pltpu.VMEM((VD, block), f32),
        pltpu.VMEM((length, KD), f32),
        pltpu.VMEM((2, stage_rows, depth), f32),
        pltpu.VMEM((2, block, depth), f32),
        pltpu.VMEM((block, depth), bf16),
        pltpu.VMEM((2, rows, depth), f32),
        pltpu.VMEM((2, rows, depth), f32),
        pltpu.VMEM((2, chips - 1, rows, LANE), f32),
        pltpu.VMEM((2, chips - 1, rows, LANE), f32),
        pltpu.VMEM((units, 1), f32),
        pltpu.VMEM((units, 1), f32),
        pltpu.VMEM((length, 1), f32),
        dma(18),
        dma(2),
        pltpu.SemaphoreType.DMA,
        dma(2),
        pltpu.SemaphoreType.DMA,
        pltpu.SemaphoreType.DMA,
        dma(2, count),
        dma(2, count),
        dma(2, count),
        dma(2, count, chips - 1),
        dma(2, count, chips - 1),
        dma(2, count, chips - 1),
        dma(2, count, chips - 1),
        dma(2, count, chips),
        dma(2, count, chips),
        dma(2, count, chips),
    ]
    return pl.pallas_call(
        functools.partial(backward_kernel, chips, quarters),
        out_shape=tuple(o for o, _ in outs),
        in_specs=[hbm] + [vmem] * 3 + [hbm] * 23,
        out_specs=tuple(s for _, s in outs),
        scratch_shapes=scratch,
        compiler_params=pltpu.CompilerParams(
            collective_id=2, has_side_effects=True, vmem_limit_bytes=VMEM_LIMIT
        ),
        cost_estimate=pl.CostEstimate(
            flops=20 * length * depth * units, bytes_accessed=80 * length * depth, transcendentals=0
        ),
    )(
        tokens, vectors, *tables, cotangent, h2, hid, md, mid, dh, gathered,
        wo, g, nh, rstd, q, k, v, wq, wk, wv, wg, h1, gated, *mlp_grads,
    )


def finish_kernel(
    chips,
    quarters,
    *refs,
):
    count = len(quarters)
    grads = refs[:count]
    part_hbm, small_ref, x_hbm, dmid_hbm, rows_ref = refs[count : count + 5]
    refs = refs[count + 5 :]
    outs = refs[:count]
    tokens_out, small_out = refs[count : count + 2]
    (late_buffer, own, sib, rcv, sacc, sbuf, part, peer, x, dmid, result, in_sem, res_sem, hs_sem, hr_sem, ss_sem, sr_sem) = refs[
        count + 2 : count + 19
    ]
    sems = refs[count + 19 :]
    ring = Ring(chips, quarters, own, sib, rcv, *sems[:5])
    late = Spread(ring, quarters, outs, late_buffer, *sems[5:10])
    bits = (2 * chips).bit_length() - 1
    f32 = jnp.float32
    block = part.shape[1]
    greet(
        [*ring.nexts, ring.peer] + [{"dp": bit_partner(ring.index, bit)} for bit in range(bits)]
    )

    ring.load(grads)

    few = block // (2 * PIECES)
    swaps = 2 * PIECES * BLOCKS

    def h_copy(n):
        i, inside = n // (2 * PIECES), pl.ds(pl.multiple_of((n % (2 * PIECES)) * few, few), few)
        return remote(part_hbm.at[i, inside, :], peer.at[i, inside, :], hs_sem.at[n], hr_sem.at[n], ring.peer)

    def h_step(n, early=False):
        if not early:
            h_copy(n - 2).wait_send()
        h_copy(n).start()

    loads = [pltpu.make_async_copy(x_hbm, x, in_sem.at[0]), pltpu.make_async_copy(dmid_hbm, dmid, in_sem.at[1])]
    for i in range(BLOCKS):
        loads.append(pltpu.make_async_copy(part_hbm.at[i, pl.ds(0, block), :], part.at[i], in_sem.at[2 + i]))

    def s_copy(level):
        target = ring.peer if level == 0 else {"dp": bit_partner(ring.index, level - 1)}
        return remote(sacc.at[level], sbuf.at[level], ss_sem.at[level], sr_sem.at[level], target)

    def s_finish(level):
        s_copy(level).wait()
        got = sbuf[level]
        if level == 0:
            first = lax.broadcasted_iota(jnp.int32, got.shape, 0) == 0
            got = jnp.where(first, got, 0.0)
        sacc[level + 1] = sacc[level] + got

    sacc[0] = small_ref[...]

    def small_step(step):
        for level in range(bits + 2):

            @pl.when(step == level)
            def _():
                if level > 0:
                    s_finish(level - 1)
                if level <= bits:
                    s_copy(level).start()

    first_order = [(ring, a) for a in range(count)]
    second_order = [(late, a) for a in range(count)]

    def first_step(step, before):
        for position, (_, a) in enumerate(first_order):
            for d in range(2):
                ring.total(grads, d, a, step, before is None)
                ring.rs_copy(d, a, step).start()
            if before is None:
                h_step(position, position < 2)
            else:
                h_step(step * len(first_order) + position)

    def rs_step(step, carry):
        first_step(step, (first_order, step - 1))

        small_step(step)
        return carry

    first_step(0, None)
    for copy in loads:
        copy.start()
    small_step(0)
    lax.fori_loop(1, chips - 1, rs_step, 0)
    for position, (_, a) in enumerate(second_order):
        for d in range(2):
            ring.total(grads, d, a, chips - 1)
            source = ring.chunk(d, a, chips - 1)
            late.ring_copy(d, a, 0, source).start()
            late.place(d, a, 0, source)
        h_step((chips - 1) * len(second_order) + position)

    each = block // PIECES
    pieces = BLOCKS * PIECES

    def token_piece(number):
        i = number // PIECES
        for n in range(2):
            h_copy(2 * number + n).wait_recv()
        inside = pl.ds(pl.multiple_of((number % PIECES) * each, each), each)
        rows = pl.ds(pl.multiple_of(number * each, each), each)
        xb = x[rows, :].astype(f32)
        r1 = lax.rsqrt(jnp.mean(xb * xb, axis=1, keepdims=True) + EPSILON)
        e = (part[i, inside, :] + peer[i, inside, :]) * rows_ref[GAIN1 : GAIN1 + 1, :]
        inner = jnp.mean(e * xb, axis=1, keepdims=True)
        result[rows, :] = low(dmid[rows, :] + r1 * e - xb * (r1 * r1 * r1 * inner))

    def ag_step(step, carry):
        for position, (_, a) in enumerate(second_order):
            for d in range(2):
                late.arrived(d, a, step - 1)
                late.ring_copy(d, a, step).start()
                late.place(d, a, step)
            number = (step - 2) * len(second_order) + position

            @pl.when((number >= 0) & (number < pieces))
            def _():
                token_piece(number)

        return carry

    for copy in loads:
        copy.wait()
    lax.fori_loop(1, chips - 1, ag_step, 0)
    tokens_copy = pltpu.make_async_copy(result, tokens_out, res_sem)
    tokens_copy.start()
    late.finish(chips - 2)
    small_out[...] = sacc[bits + 1]
    ring.drain_ring()
    late.drain_ring()
    ring.drain_pair(grads)
    late.drain()
    for n in range(swaps - 2, swaps):
        h_copy(n).wait_send()
    tokens_copy.wait()


def finish(grads, part, small, tokens, dmid, vectors):
    chips = lax.axis_size("dp") // 2
    length, depth = tokens.shape
    block = length // BLOCKS
    quarters = tuple(g.shape[0] // 4 for g in grads)
    rows = sum(quarters)
    count = len(quarters)
    bits = (2 * chips).bit_length() - 1
    f32, bf16 = jnp.float32, jnp.bfloat16
    vmem = pl.BlockSpec(memory_space=pltpu.VMEM)
    hbm = pl.BlockSpec(memory_space=pl.ANY)
    dma = lambda *shape: pltpu.SemaphoreType.DMA(shape)
    shape = jax.ShapeDtypeStruct
    outs = [(shape(g.shape, f32), hbm) for g in grads]
    outs += [
        (shape((length, depth), bf16), hbm),
        (shape(small.shape, f32), vmem),
    ]
    scratch = [
        pltpu.VMEM((2, chips - 1, rows, LANE), f32),
        pltpu.VMEM((2, rows, depth), f32),
        pltpu.VMEM((2, rows, depth), f32),
        pltpu.VMEM((2, chips - 1, rows, LANE), f32),
        pltpu.VMEM((bits + 2, *small.shape), f32),
        pltpu.VMEM((bits + 1, *small.shape), f32),
        pltpu.VMEM((BLOCKS, block, depth), f32),
        pltpu.VMEM((BLOCKS, block, depth), f32),
        pltpu.VMEM((length, depth), bf16),
        pltpu.VMEM((length, depth), f32),
        pltpu.VMEM((length, depth), bf16),
        dma(2 + BLOCKS),
        pltpu.SemaphoreType.DMA,
        dma(2 * PIECES * BLOCKS),
        dma(2 * PIECES * BLOCKS),
        dma(bits + 1),
        dma(bits + 1),
        dma(2, count),
        dma(2, count),
        dma(2, count),
        dma(2, count, chips - 1),
        dma(2, count, chips - 1),
    ]
    scratch += [
        dma(2, count, chips - 1),
        dma(2, count, chips - 1),
        dma(2, count, chips),
        dma(2, count, chips),
        dma(2, count, chips),
    ]
    return pl.pallas_call(
        functools.partial(finish_kernel, chips, quarters),
        out_shape=tuple(o for o, _ in outs),
        in_specs=[hbm] * (count + 1) + [vmem] + [hbm] * 2 + [vmem],
        out_specs=tuple(s for _, s in outs),
        scratch_shapes=scratch,
        compiler_params=pltpu.CompilerParams(
            collective_id=3, has_side_effects=True, vmem_limit_bytes=VMEM_LIMIT
        ),
        cost_estimate=pl.CostEstimate(
            flops=20 * rows * depth, bytes_accessed=80 * rows * depth, transcendentals=0
        ),
    )(*grads, part, small, tokens, dmid, vectors)


def deliver_kernel(count, key_width, *refs):
    sources, targets = refs[:count], refs[count : 2 * count + 1]
    buffer, low_buffer, in_sem, out_sem = refs[2 * count + 1 :]
    pieces = []
    for a in range(count):
        parts = DELIVER if sources[a].dtype == jnp.float32 else 1
        rows = sources[a].shape[0] // parts
        for n in range(parts):
            pieces.append((a, pl.ds(n * rows, rows), rows))
    wide = sum(sources[a].dtype == jnp.float32 for a, _, _ in pieces)
    low_start = [sum(r for _, _, r in pieces[wide:n]) for n in range(wide, len(pieces))]

    def spot(number):
        rows = pieces[number][2]
        if number < wide:
            return buffer.at[number, pl.ds(0, rows), :]
        return low_buffer.at[pl.ds(low_start[number - wide], rows), :]

    def load(number):
        a, where, rows = pieces[number]
        return pltpu.make_async_copy(sources[a].at[where, :], spot(number), in_sem.at[number])

    def stores(number):
        a, where, rows = pieces[number]
        if a:
            spots = [(spot(number), targets[a + 1].at[where, :])]
        else:
            spots = [
                (buffer.at[number, pl.ds(0, rows), pl.ds(half * key_width, key_width)], targets[half].at[where, :])
                for half in range(2)
            ]
        return [pltpu.make_async_copy(s, t, out_sem.at[number, n]) for n, (s, t) in enumerate(spots)]

    for number in range(len(pieces)):
        load(number).start()
    for number in range(len(pieces)):
        load(number).wait()
        for copy in stores(number):
            copy.start()
    for number in range(len(pieces)):
        for copy in stores(number):
            copy.wait()


def deliver(arrays, narrow, key_width):
    hbm = pl.BlockSpec(memory_space=pl.ANY)
    every = (*arrays, *narrow)
    shapes = [((arrays[0].shape[0], key_width), jnp.float32)] * 2 + [(a.shape, a.dtype) for a in every[1:]]
    size = sum(a.size for a in arrays)
    wide = DELIVER * len(arrays)
    pieces = wide + len(narrow)
    depth = arrays[0].shape[1]
    rows = max(a.shape[0] for a in arrays) // DELIVER
    return pl.pallas_call(
        functools.partial(deliver_kernel, len(every), key_width),
        out_shape=tuple(jax.ShapeDtypeStruct(s, t) for s, t in shapes),
        in_specs=[hbm] * len(every),
        out_specs=(hbm,) * len(shapes),
        scratch_shapes=[
            pltpu.VMEM((wide, rows, depth), jnp.float32),
            pltpu.VMEM((sum(a.shape[0] for a in narrow), depth), jnp.bfloat16),
            pltpu.SemaphoreType.DMA((pieces,)),
            pltpu.SemaphoreType.DMA((pieces, 2)),
        ],
        compiler_params=pltpu.CompilerParams(vmem_limit_bytes=56 * 1024 * 1024),
        cost_estimate=pl.CostEstimate(flops=0, bytes_accessed=8 * size, transcendentals=0),
    )(*every)

def swap(array):
    return lax.ppermute(array, "tensor", [(0, 1), (1, 0)])


def other_half(arrays, zero):
    dp, index = lax.axis_size("dp"), lax.axis_index("dp")
    rows = arrays[0].shape[0]
    count = len(arrays)
    if dp % count == 0 and rows % (8 * (dp // count)) == 0:
        share = rows * count // dp
        each = dp // count
        inside = (index % each) * share
        own = [lax.dynamic_slice_in_dim(a, inside, share, 0) for a in arrays]
        part = own[0]
        for number in range(1, count):
            part = jnp.where(index // each == number, own[number], part)
    else:
        share = -(-rows * count // (8 * dp)) * 8
        whole = jnp.concatenate(arrays, axis=0)
        whole = jnp.pad(whole, ((0, share * dp - rows * count), (0, 0)))
        part = lax.dynamic_slice_in_dim(whole, index * share, share, 0)
    got = lax.all_gather(swap(part.astype(jnp.float32)), "dp", axis=0, tiled=True)
    got = low(got + zero)
    return [got[number * rows : (number + 1) * rows] for number in range(count)]


def plain_body(
    tokens,
    segment,
    norm1_gain,
    w_query,
    w_key,
    w_value,
    w_gate,
    group_gain,
    group_bias,
    w_out,
    norm2_gain,
    w_mlp_gate,
    w_mlp_up,
    w_mlp_down,
    cotangent,
):
    length, depth = tokens.shape
    heads = w_query.shape[1] // KD
    block = length // BLOCKS
    tensor = lax.axis_index("tensor")
    f32 = jnp.float32
    zero = jnp.minimum(segment[0], 0).astype(f32)
    value_t, gate_t, mg_t, mu_t = w_value.T, w_gate.T, w_mlp_gate.T, w_mlp_up.T
    mg_o, mu_o, md_o, wo_o = other_half([mg_t, mu_t, w_mlp_down, w_out], zero)
    x = tokens.astype(f32)
    gain1 = norm1_gain.astype(f32)
    gain2 = norm2_gain.astype(f32)
    ggain = group_gain.astype(f32)[:, None]
    gbias = group_bias.astype(f32)[:, None]
    r1 = lax.rsqrt(jnp.mean(x * x, axis=1, keepdims=True) + EPSILON)
    h1 = low(x * r1 * gain1)
    half = KD // 2
    frequency = jnp.exp(-jnp.log(10000.0) * jnp.arange(half, dtype=f32) / half)
    angles = jnp.arange(length, dtype=f32)[:, None] * frequency[None, :]
    cosine, sine = jnp.cos(angles), jnp.sin(angles)
    positions = jnp.arange(length, dtype=jnp.int32)
    visible = (positions[:, None] >= positions[None, :]) & (segment[:, None] == segment[None, :])
    offsets = jnp.maximum(positions[:, None] - positions[None, :], 0).astype(f32)

    def decay(head, rows, columns):
        order = (tensor * heads + head).astype(f32)
        rate = jnp.log1p(-jnp.exp2(-5.0 - order))
        return jnp.where(visible[rows, columns], jnp.exp(offsets[rows, columns] * rate), 0.0)

    queries = [[] for _ in range(heads)]
    keys = [[] for _ in range(heads)]
    values = [[] for _ in range(heads)]
    gates = [[] for _ in range(heads)]
    nhats = [[] for _ in range(heads)]
    spreads = [[] for _ in range(heads)]
    gated_blocks, received = [], []
    for number in range(BLOCKS):
        rows = slice(number * block, (number + 1) * block)
        seen = slice(0, (number + 1) * block)
        own = []
        for head in range(heads):
            wide = slice(head * KD, (head + 1) * KD)
            tall = slice(head * VD, (head + 1) * VD)
            q = low(turn(dot(h1[rows], w_query[:, wide], 1, 0), cosine[rows], sine[rows]))
            k = turn(dot(h1[rows], w_key[:, wide], 1, 0), cosine[rows], sine[rows])
            queries[head].append(q)
            keys[head].append(low(k * KD ** (-0.5)))
            values[head].append(low(dot(value_t[tall], h1[rows], 1, 1)))
            g = dot(gate_t[tall], h1[rows], 1, 1)
            gates[head].append(g)
            scores = dot(q, jnp.concatenate(keys[head], axis=0), 1, 1)
            scores = low(scores * decay(head, rows, seen))
            ret = dot(jnp.concatenate(values[head], axis=1), scores, 1, 1)
            centred = ret - jnp.mean(ret, axis=0, keepdims=True)
            scale = lax.rsqrt(jnp.mean(centred * centred, axis=0, keepdims=True) + GROUP_EPSILON)
            nhat = centred * scale
            nhats[head].append(nhat)
            spreads[head].append(scale)
            own.append(low(jax.nn.silu(g) * (nhat * ggain[tall] + gbias[tall])))
        gated_blocks.append(jnp.concatenate(own, axis=0))
        received.append(low(swap(gated_blocks[-1].astype(f32)) + zero))

    mids, h2s, r2s, hidden_own, hidden_oth, das, dbs, dmids = [], [], [], [], [], [], [], []
    norm2_rows = []
    for number in range(BLOCKS):
        rows = slice(number * block, (number + 1) * block)
        mid = x[rows] + (dot(gated_blocks[number], w_out, 0, 0) + dot(received[number], wo_o, 0, 0))
        r2 = lax.rsqrt(jnp.mean(mid * mid, axis=1, keepdims=True) + EPSILON)
        h2 = low(mid * r2 * gain2)
        cot = cotangent[rows]

        def mlp(gate_w, up_w, down_w):
            a, b = dot(gate_w, h2, 1, 1), dot(up_w, h2, 1, 1)
            hidden, pull = jax.vjp(lambda s, t: jax.nn.gelu(s) * t, a, b)
            da, db = pull(dot(down_w, cot, 1, 1))
            da, db = low(da), low(db)
            return low(hidden), da, db, dot(da, gate_w, 0, 0) + dot(db, up_w, 0, 0)

        own_hidden, da, db, part = mlp(mg_t, mu_t, w_mlp_down)
        oth_hidden, _, _, more = mlp(mg_o, mu_o, md_o)
        dh2 = part + more
        e = dh2 * gain2
        dmid = cot.astype(f32) + r2 * e - mid * (r2 * r2 * r2) * jnp.mean(e * mid, axis=1, keepdims=True)
        norm2_rows.append(jnp.sum(dh2 * mid * r2, axis=0))
        for where, value in zip(
            (mids, h2s, hidden_own, hidden_oth, das, dbs, dmids),
            (mid, h2, own_hidden, oth_hidden, da, db, dmid),
        ):
            where.append(value)
    grad_norm2 = sum(norm2_rows)
    mid = jnp.concatenate(mids, axis=0)
    h2 = jnp.concatenate(h2s, axis=0)
    hidden = jnp.concatenate(hidden_own, axis=1)
    hidden_o = jnp.concatenate(hidden_oth, axis=1)
    dmid = jnp.concatenate(dmids, axis=0)
    own_rows = length // lax.axis_size("tensor")
    place = tensor * own_rows
    output = low(
        lax.dynamic_slice_in_dim(mid, place, own_rows, 0)
        + dot(lax.dynamic_slice_in_dim(hidden, place, own_rows, 1), w_mlp_down, 0, 0)
        + dot(lax.dynamic_slice_in_dim(hidden_o, place, own_rows, 1), md_o, 0, 0)
    )
    grad_mg = dot(jnp.concatenate(das, axis=1), h2, 1, 0)
    grad_mu = dot(jnp.concatenate(dbs, axis=1), h2, 1, 0)
    grad_md = dot(hidden, cotangent, 1, 0)

    branch = low(dmid)
    gated = jnp.concatenate(gated_blocks, axis=1)
    grad_out = dot(gated, branch, 1, 0)
    dgated = dot(w_out, branch, 1, 1)
    dqs, dks, dvs, dgs, ggains, gbiases = [], [], [], [], [], []
    everything = slice(0, length)
    for head in range(heads):
        tall = slice(head * VD, (head + 1) * VD)
        g = jnp.concatenate(gates[head], axis=1)
        nhat = jnp.concatenate(nhats[head], axis=1)
        spread = jnp.concatenate(spreads[head], axis=1)
        q = jnp.concatenate(queries[head], axis=0)
        k = jnp.concatenate(keys[head], axis=0)
        v = jnp.concatenate(values[head], axis=1)
        sigmoid = jax.nn.sigmoid(g)
        silu = g * sigmoid
        up = dgated[tall]
        dgn = up * silu
        ggains.append(jnp.sum(dgn * nhat, axis=1))
        gbiases.append(jnp.sum(dgn, axis=1))
        f = dgn * ggain[tall]
        dret = (
            f - jnp.mean(f, axis=0, keepdims=True) - nhat * jnp.mean(f * nhat, axis=0, keepdims=True)
        ) * spread
        dret = low(dret)
        gn = nhat * ggain[tall] + gbias[tall]
        dgs.append(low(up * gn * (sigmoid + silu * (1.0 - sigmoid))))
        table = decay(head, everything, everything)
        scores = low(dot(q, k, 1, 1) * table)
        draw = low(dot(dret, v, 0, 0) * table)
        dvs.append(low(dot(dret, scores, 1, 0)))
        dqs.append(low(turn(dot(draw, k, 1, 0), cosine, -sine)))
        dks.append(low(turn(dot(draw, q, 0, 0), cosine, -sine) * KD ** (-0.5)))
    dv = jnp.concatenate(dvs, axis=0)
    dg = jnp.concatenate(dgs, axis=0)
    dq = jnp.concatenate(dqs, axis=1)
    dk = jnp.concatenate(dks, axis=1)
    partial_in = dot(dq, w_query, 1, 1) + dot(dk, w_key, 1, 1) + dot(dv, value_t, 0, 0) + dot(dg, gate_t, 0, 0)
    grad_norm1 = jnp.sum(partial_in * x * r1, axis=0)
    grad_qk = dot(h1, jnp.concatenate([dq, dk], axis=1), 0, 0)
    grad_v = dot(dv, h1, 1, 0)
    grad_g = dot(dg, h1, 1, 0)

    units = w_value.shape[1]
    small = jnp.stack(
        [
            grad_norm1,
            grad_norm2,
            jnp.pad(jnp.concatenate(ggains), (0, depth - units)),
            jnp.pad(jnp.concatenate(gbiases), (0, depth - units)),
        ]
    )
    small = jnp.pad(small, ((0, 4), (0, 0)))
    grads = lax.psum((grad_qk, grad_v, grad_g, grad_out, grad_mg, grad_mu, grad_md), "dp")
    peer = swap(partial_in)
    small = lax.psum(small.at[0].set(lax.psum(small[0], "tensor")), "dp")
    grad_qk, grad_v, grad_g, grad_out, grad_mg, grad_mu, grad_md = grads
    e1 = (partial_in + peer) * gain1
    grad_tokens = low(dmid + r1 * e1 - x * (r1 * r1 * r1) * jnp.mean(e1 * x, axis=1, keepdims=True))
    key_width = w_query.shape[1]
    return (
        output,
        grad_tokens,
        small[0],
        grad_qk[:, :key_width],
        grad_qk[:, key_width:],
        grad_v.T,
        grad_g.T,
        small[2, :units],
        small[3, :units],
        grad_out,
        small[1],
        grad_mg.T,
        grad_mu.T,
        grad_md,
    )


def body(
    tokens,
    segment,
    norm1_gain,
    w_query,
    w_key,
    w_value,
    w_gate,
    group_gain,
    group_bias,
    w_out,
    norm2_gain,
    w_mlp_gate,
    w_mlp_up,
    w_mlp_down,
    cotangent,
):
    length, depth = tokens.shape
    if depth % (LANE * (lax.axis_size("dp") // 2)):
        return plain_body(
            tokens, segment, norm1_gain, w_query, w_key, w_value, w_gate, group_gain, group_bias, w_out,
            norm2_gain, w_mlp_gate, w_mlp_up, w_mlp_down, cotangent,
        )
    value_t, gate_t, mg_t, mu_t = w_value.T, w_gate.T, w_mlp_gate.T, w_mlp_up.T
    tables = make_tables(length)
    vectors = pack_rows((norm1_gain, norm2_gain, group_gain, group_bias, segment), depth)
    (h1, qs, ks, vs, g, nhat, rstd, gated, mid, dh, h2, hid, grad_mg, grad_mu, grad_md, gathered) = forward(
        tokens,
        vectors,
        tables,
        (w_query, w_key, value_t, gate_t, w_out, mg_t, mu_t, w_mlp_down),
        cotangent,
    )
    (dmid, output, grad_mg, grad_mu, grad_md, part, grad_qk, grad_v, grad_g, grad_out, small) = backward(
        tokens,
        vectors,
        tables,
        cotangent,
        (mid, dh, h2, hid, gathered),
        (h1, qs, ks, vs, g, nhat, rstd, gated),
        (w_query, w_key, value_t, gate_t, w_out, w_mlp_down),
        (grad_mg, grad_mu, grad_md),
    )
    (grad_qk, grad_v, grad_g, grad_out, grad_tokens, small) = finish(
        (grad_qk, grad_v, grad_g, grad_out), part, small, tokens, dmid, vectors
    )
    units = w_value.shape[1]
    grad_q, grad_k, grad_v, grad_g, grad_out, grad_mg, grad_mu, grad_md, output, grad_tokens = deliver(
        (grad_qk, grad_v, grad_g, grad_out, grad_mg, grad_mu, grad_md), (output, grad_tokens), w_query.shape[1]
    )
    return (
        output,
        grad_tokens,
        small[0],
        grad_q,
        grad_k,
        grad_v.T,
        grad_g.T,
        small[2, :units],
        small[3, :units],
        grad_out,
        small[1],
        grad_mg.T,
        grad_mu.T,
        grad_md,
    )


def solution(mesh):
    placed = (
        P("dp", None),
        P("dp"),
        P(),
        P(None, "tensor"),
        P(None, "tensor"),
        P(None, "tensor"),
        P(None, "tensor"),
        P("tensor"),
        P("tensor"),
        P("tensor", None),
        P(),
        P(None, "tensor"),
        P(None, "tensor"),
        P("tensor", None),
        P("dp", None),
    )
    return jax.shard_map(
        body,
        mesh=mesh,
        in_specs=placed,
        out_specs=(
            P(("dp", "tensor"), None),
            P("dp", None),
            P(),
            P(None, "tensor"),
            P(None, "tensor"),
            P(None, "tensor"),
            P(None, "tensor"),
            P("tensor"),
            P("tensor"),
            P("tensor", None),
            P(),
            P(None, "tensor"),
            P(None, "tensor"),
            P("tensor", None),
        ),
        check_vma=False,
    )
```

profile of v0, /device:TPU:0, one launch (start us, length us, event | category | flops | bytes accessed | tf_op | source)
XLA Modules:
  0.0 432.2 jit_solution(11939153206999517441)
XLA Ops:
  0.6 0.7 convert_element_type.6
  1.3 0.7 stack.40
  2.0 0.7 pad_convert_fusion.1
  2.7 0.7 pad_convert_fusion
  3.4 0.7 stack.41
  4.1 0.6 pad.15.rows_ref.refs_8_
  4.7 114.3 %shard_map.272 = (bf16[1024,1024]{1,0:T(8,128)(2,1)}, bf16[2,1024,256]{2,1,0:T(8,128)(2,1)}, bf16[2,1024,256]{2,1,0:T(8,128)(2,1)}, bf16[864,1024]{1,0:T(8,128)(...) custom-call(bf16[1024,1024]{1,0:T(8,128)(2,1)} %refs_6_.1, ...), custom_call_target="tpu_custom_call" | custom-call | flops 36238786560 | bytes 83886080 | tf_op jit(solution)/shard_map/pallas_call | solution.py:585
  119.1 129.5 %shard_map.273 = (f32[1024,1024]{1,0:T(8,128)}, bf16[512,1024]{1,0:T(8,128)(2,1)}, f32[864,1024]{1,0:T(8,128)}, f32[864,1024]{1,0:T(8,128)}, f32[864,1024]{1,0:T...) custom-call(bf16[1024,1024]{1,0:T(8,128)(2,1)} %refs_6_.1, ...), custom_call_target="tpu_custom_call" | custom-call | flops 18119393280 | bytes 83886080 | tf_op jit(solution)/shard_map/pallas_call | solution.py:1226
  248.6 160.0 %shard_map.274 = (f32[1024,1024]{1,0:T(8,128)}, f32[864,1024]{1,0:T(8,128)}, f32[864,1024]{1,0:T(8,128)}, f32[864,1024]{1,0:T(8,128)}, bf16[1024,1024]{1,0:T(8,128)(2,1)}, /*index=5*/f32[8,1024]{1,0:T(8,128)}) custom-call(f32[1024,1024]{1,0:T(8,128)} %get-tuple-element.73.refs_0_, f32[864,1024]{1,0:T(8,128)} %get-tuple-element.74.refs_1_, ...), custom_call_target="tpu_custom_call" | custom-call | flops 18513920 | bytes 74055680 | tf_op jit(solution)/shard_map/pallas_call | solution.py:1436
  408.5 20.3 %shard_map.275 = (f32[1024,512]{1,0:T(8,128)}, f32[1024,512]{1,0:T(8,128)}, f32[864,1024]{1,0:T(8,128)}, f32[864,1024]{1,0:T(8,128)}, f32[864,1024]{1,0:T(8,128)...) custom-call(f32[1024,1024]{1,0:T(8,128)} %get-tuple-element.80.refs_, ...), custom_call_target="tpu_custom_call" | custom-call | bytes 50855936 | tf_op jit(solution)/shard_map/pallas_call | solution.py:1504
  428.9 1.4 fusion
  430.3 1.4 slice_reduce_fusion
  (1 shorter events, 0.0 us)
where the time goes:
time: 439 us; the launch traced here: 432 us
  Pallas kernels  424 us (97%)
    pallas_call x1, Pallas kernels, finish(): pl.pallas_call(functools.partial(finish_kernel, chips, quarters), out_sha...  160 us
    pallas_call x1, Pallas kernels, backward(): pl.pallas_call(functools.partial(backward_kernel, chips, quarters), out_s...  129 us
    pallas_call x1, Pallas kernels, forward(): pl.pallas_call(functools.partial(forward_kernel, chips), out_shape=tuple(...  114 us
    pallas_call x1, Pallas kernels, deliver(): pl.pallas_call(functools.partial(deliver_kernel, len(every), key_width),...  20.3 us

commit v1 on v0

--- a/solution.py
+++ b/solution.py
@@ -15,6 +15,7 @@
 MESH = pl.DeviceIdType.MESH
 DELIVER = 4
 PIECES = 4
+LAG = 8
 VMEM_LIMIT = 63 * 1024 * 1024
 
 
@@ -1025,10 +1026,10 @@
             nh[tall, rows] = low((f - mean - nhat * inner) * rstd[head : head + 1, rows])
             gn = nhat * gain + gbias_ref[tall, :]
             g[tall, rows] = low(up * gn * (sigmoid + silu * (1.0 - sigmoid)))
+            pump()
 
     for i in range(BLOCKS):
         gate_block(i)
-        pump()
     for copy in (copies[7], copies[8], copies[12]):
         copy.wait()
 
@@ -1095,7 +1096,9 @@
                 more = dot(values[head, rows, :], weights[:, wide], 1, 1)
                 total = more if total is None else total + more
         stage[slot, 0:block, :] = total
+        pump()
         stage[slot, 0:block, :] += dot(v[:, rows], wv[...], 0, 0)
+        pump()
         stage[slot, 0:block, :] += dot(g[:, rows], wg[...], 0, 0)
         xb = x[rows, :].astype(f32)
         r1 = lax.rsqrt(jnp.mean(xb * xb, axis=1, keepdims=True) + EPSILON)
@@ -1310,15 +1313,51 @@
     first_order = [(ring, a) for a in range(count)]
     second_order = [(late, a) for a in range(count)]
 
+    each = block // PIECES
+    pieces = BLOCKS * PIECES
+
+    def token_piece(number):
+        i = number // PIECES
+        for n in range(2):
+            h_copy(2 * number + n).wait_recv()
+
+        @pl.when(number == 0)
+        def _():
+            for copy in loads:
+                copy.wait()
+
+        inside = pl.ds(pl.multiple_of((number % PIECES) * each, each), each)
+        rows = pl.ds(pl.multiple_of(number * each, each), each)
+        xb = x[rows, :].astype(f32)
+        r1 = lax.rsqrt(jnp.mean(xb * xb, axis=1, keepdims=True) + EPSILON)
+        e = (part[i, inside, :] + peer[i, inside, :]) * rows_ref[GAIN1 : GAIN1 + 1, :]
+        inner = jnp.mean(e * xb, axis=1, keepdims=True)
+        result[rows, :] = low(dmid[rows, :] + r1 * e - xb * (r1 * r1 * r1 * inner))
+
+    def when(condition, action):
+        if isinstance(condition, bool):
+            if condition:
+                action()
+        else:
+            pl.when(condition)(action)
+
+    def beside(turn):
+        piece = (turn // 3) * 2 + turn % 3
+        late_turn = turn - LAG
+        if isinstance(turn, int):
+            when(turn % 3 != 2 and piece < swaps, lambda: h_step(piece, piece < 2))
+            when(late_turn >= 0 and late_turn % 3 == 0, lambda: token_piece(late_turn // 3))
+        else:
+            when((turn % 3 != 2) & (piece < swaps), lambda: h_step(piece))
+            ready = (late_turn >= 0) & (late_turn % 3 == 0) & (late_turn // 3 < pieces)
+            when(ready, lambda: token_piece(late_turn // 3))
+
     def first_step(step, before):
         for position, (_, a) in enumerate(first_order):
             for d in range(2):
                 ring.total(grads, d, a, step, before is None)
                 ring.rs_copy(d, a, step).start()
-            if before is None:
-                h_step(position, position < 2)
-            else:
-                h_step(step * len(first_order) + position)
+            beside(step * count + position)
 
     def rs_step(step, carry):
         first_step(step, (first_order, step - 1))
@@ -1337,22 +1376,7 @@
             source = ring.chunk(d, a, chips - 1)
             late.ring_copy(d, a, 0, source).start()
             late.place(d, a, 0, source)
-        h_step((chips - 1) * len(second_order) + position)
-
-    each = block // PIECES
-    pieces = BLOCKS * PIECES
-
-    def token_piece(number):
-        i = number // PIECES
-        for n in range(2):
-            h_copy(2 * number + n).wait_recv()
-        inside = pl.ds(pl.multiple_of((number % PIECES) * each, each), each)
-        rows = pl.ds(pl.multiple_of(number * each, each), each)
-        xb = x[rows, :].astype(f32)
-        r1 = lax.rsqrt(jnp.mean(xb * xb, axis=1, keepdims=True) + EPSILON)
-        e = (part[i, inside, :] + peer[i, inside, :]) * rows_ref[GAIN1 : GAIN1 + 1, :]
-        inner = jnp.mean(e * xb, axis=1, keepdims=True)
-        result[rows, :] = low(dmid[rows, :] + r1 * e - xb * (r1 * r1 * r1 * inner))
+        beside((chips - 1) * count + position)
 
     def ag_step(step, carry):
         for position, (_, a) in enumerate(second_order):
@@ -1360,16 +1384,10 @@
                 late.arrived(d, a, step - 1)
                 late.ring_copy(d, a, step).start()
                 late.place(d, a, step)
-            number = (step - 2) * len(second_order) + position
-
-            @pl.when((number >= 0) & (number < pieces))
-            def _():
-                token_piece(number)
+            beside((chips - 1 + step) * count + position)
 
         return carry
 
-    for copy in loads:
-        copy.wait()
     lax.fori_loop(1, chips - 1, ag_step, 0)
     tokens_copy = pltpu.make_async_copy(result, tokens_out, res_sem)
     tokens_copy.start()

time: 439 us -> 444 us (1.011)
  Pallas kernels: 424 us -> 429 us
    pallas_call x1, Pallas kernels: 129 us -> 140 us  [backward(): pl.pallas_call(functools.partial(backward_kernel, chips, quarters), out_s...]
    pallas_call x1, Pallas kernels: 160 us -> 155 us  [finish(): pl.pallas_call(functools.partial(finish_kernel, chips, quarters), out_sha...]
where the time goes in v1:
time: 444 us; the launch traced here: 437 us
  Pallas kernels  429 us (97%)
    pallas_call x1, Pallas kernels, finish(): pl.pallas_call(functools.partial(finish_kernel, chips, quarters), out_sha...  155 us
    pallas_call x1, Pallas kernels, backward(): pl.pallas_call(functools.partial(backward_kernel, chips, quarters), out_s...  140 us
    pallas_call x1, Pallas kernels, forward(): pl.pallas_call(functools.partial(forward_kernel, chips), out_shape=tuple(...  114 us
    pallas_call x1, Pallas kernels, deliver(): pl.pallas_call(functools.partial(deliver_kernel, len(every), key_width),...  20.3 us

profile of v1, /device:TPU:0, one launch (start us, length us, event | category | flops | bytes accessed | tf_op | source)
XLA Modules:
  0.0 437.3 jit_solution(4503726752903242335)
XLA Ops:
  0.6 0.7 convert_element_type.6
  1.3 0.7 stack.40
  2.0 0.7 pad_convert_fusion.1
  2.7 0.7 pad_convert_fusion
  3.4 0.7 stack.41
  4.1 0.6 pad.15.rows_ref.refs_8_
  4.7 114.3 %shard_map.272 = (bf16[1024,1024]{1,0:T(8,128)(2,1)}, bf16[2,1024,256]{2,1,0:T(8,128)(2,1)}, bf16[2,1024,256]{2,1,0:T(8,128)(2,1)}, bf16[864,1024]{1,0:T(8,128)(...) custom-call(bf16[1024,1024]{1,0:T(8,128)(2,1)} %refs_6_.1, ...), custom_call_target="tpu_custom_call" | custom-call | flops 36238786560 | bytes 83886080 | tf_op jit(solution)/shard_map/pallas_call | solution.py:586
  119.1 139.9 %shard_map.273 = (f32[1024,1024]{1,0:T(8,128)}, bf16[512,1024]{1,0:T(8,128)(2,1)}, f32[864,1024]{1,0:T(8,128)}, f32[864,1024]{1,0:T(8,128)}, f32[864,1024]{1,0:T...) custom-call(bf16[1024,1024]{1,0:T(8,128)(2,1)} %refs_6_.1, ...), custom_call_target="tpu_custom_call" | custom-call | flops 18119393280 | bytes 83886080 | tf_op jit(solution)/shard_map/pallas_call | solution.py:1229
  259.0 154.6 %shard_map.274 = (f32[1024,1024]{1,0:T(8,128)}, f32[864,1024]{1,0:T(8,128)}, f32[864,1024]{1,0:T(8,128)}, f32[864,1024]{1,0:T(8,128)}, bf16[1024,1024]{1,0:T(8,128)(2,1)}, /*index=5*/f32[8,1024]{1,0:T(8,128)}) custom-call(f32[1024,1024]{1,0:T(8,128)} %get-tuple-element.73.refs_0_, f32[864,1024]{1,0:T(8,128)} %get-tuple-element.74.refs_1_, ...), custom_call_target="tpu_custom_call" | custom-call | flops 18513920 | bytes 74055680 | tf_op jit(solution)/shard_map/pallas_call | solution.py:1454
  413.6 20.3 %shard_map.275 = (f32[1024,512]{1,0:T(8,128)}, f32[1024,512]{1,0:T(8,128)}, f32[864,1024]{1,0:T(8,128)}, f32[864,1024]{1,0:T(8,128)}, f32[864,1024]{1,0:T(8,128)...) custom-call(f32[1024,1024]{1,0:T(8,128)} %get-tuple-element.80.refs_, ...), custom_call_target="tpu_custom_call" | custom-call | bytes 50855936 | tf_op jit(solution)/shard_map/pallas_call | solution.py:1522
  433.9 1.4 fusion
  435.4 1.4 slice_reduce_fusion
  (1 shorter events, 0.0 us)

commit v2 on v1

--- a/solution.py
+++ b/solution.py
@@ -1026,10 +1026,10 @@
             nh[tall, rows] = low((f - mean - nhat * inner) * rstd[head : head + 1, rows])
             gn = nhat * gain + gbias_ref[tall, :]
             g[tall, rows] = low(up * gn * (sigmoid + silu * (1.0 - sigmoid)))
-            pump()
 
     for i in range(BLOCKS):
         gate_block(i)
+        pump()
     for copy in (copies[7], copies[8], copies[12]):
         copy.wait()
 
@@ -1096,9 +1096,7 @@
                 more = dot(values[head, rows, :], weights[:, wide], 1, 1)
                 total = more if total is None else total + more
         stage[slot, 0:block, :] = total
-        pump()
         stage[slot, 0:block, :] += dot(v[:, rows], wv[...], 0, 0)
-        pump()
         stage[slot, 0:block, :] += dot(g[:, rows], wg[...], 0, 0)
         xb = x[rows, :].astype(f32)
         r1 = lax.rsqrt(jnp.mean(xb * xb, axis=1, keepdims=True) + EPSILON)

time: 444 us -> 434 us (0.977)
  Pallas kernels: 429 us -> 419 us
    pallas_call x1, Pallas kernels: 140 us -> 129 us  [backward(): pl.pallas_call(functools.partial(backward_kernel, chips, quarters), out_s...]
where the time goes in v2:
time: 434 us; the launch traced here: 427 us
  Pallas kernels  419 us (97%)
    pallas_call x1, Pallas kernels, finish(): pl.pallas_call(functools.partial(finish_kernel, chips, quarters), out_sha...  155 us
    pallas_call x1, Pallas kernels, backward(): pl.pallas_call(functools.partial(backward_kernel, chips, quarters), out_s...  129 us
    pallas_call x1, Pallas kernels, forward(): pl.pallas_call(functools.partial(forward_kernel, chips), out_shape=tuple(...  114 us
    pallas_call x1, Pallas kernels, deliver(): pl.pallas_call(functools.partial(deliver_kernel, len(every), key_width),...  20.3 us

profile of v2, /device:TPU:0, one launch (start us, length us, event | category | flops | bytes accessed | tf_op | source)
XLA Modules:
  0.0 426.8 jit_solution(11760331760322405964)
XLA Ops:
  0.6 0.7 convert_element_type.6
  1.3 0.7 stack.40
  2.0 0.7 pad_convert_fusion.1
  2.7 0.7 pad_convert_fusion
  3.4 0.7 stack.41
  4.1 0.6 pad.15.rows_ref.refs_8_
  4.7 114.3 %shard_map.272 = (bf16[1024,1024]{1,0:T(8,128)(2,1)}, bf16[2,1024,256]{2,1,0:T(8,128)(2,1)}, bf16[2,1024,256]{2,1,0:T(8,128)(2,1)}, bf16[864,1024]{1,0:T(8,128)(...) custom-call(bf16[1024,1024]{1,0:T(8,128)(2,1)} %refs_6_.1, ...), custom_call_target="tpu_custom_call" | custom-call | flops 36238786560 | bytes 83886080 | tf_op jit(solution)/shard_map/pallas_call | solution.py:586
  119.1 129.5 %shard_map.273 = (f32[1024,1024]{1,0:T(8,128)}, bf16[512,1024]{1,0:T(8,128)(2,1)}, f32[864,1024]{1,0:T(8,128)}, f32[864,1024]{1,0:T(8,128)}, f32[864,1024]{1,0:T...) custom-call(bf16[1024,1024]{1,0:T(8,128)(2,1)} %refs_6_.1, ...), custom_call_target="tpu_custom_call" | custom-call | flops 18119393280 | bytes 83886080 | tf_op jit(solution)/shard_map/pallas_call | solution.py:1227
  248.6 154.6 %shard_map.274 = (f32[1024,1024]{1,0:T(8,128)}, f32[864,1024]{1,0:T(8,128)}, f32[864,1024]{1,0:T(8,128)}, f32[864,1024]{1,0:T(8,128)}, bf16[1024,1024]{1,0:T(8,128)(2,1)}, /*index=5*/f32[8,1024]{1,0:T(8,128)}) custom-call(f32[1024,1024]{1,0:T(8,128)} %get-tuple-element.73.refs_0_, f32[864,1024]{1,0:T(8,128)} %get-tuple-element.74.refs_1_, ...), custom_call_target="tpu_custom_call" | custom-call | flops 18513920 | bytes 74055680 | tf_op jit(solution)/shard_map/pallas_call | solution.py:1452
  403.2 20.3 %shard_map.275 = (f32[1024,512]{1,0:T(8,128)}, f32[1024,512]{1,0:T(8,128)}, f32[864,1024]{1,0:T(8,128)}, f32[864,1024]{1,0:T(8,128)}, f32[864,1024]{1,0:T(8,128)...) custom-call(f32[1024,1024]{1,0:T(8,128)} %get-tuple-element.80.refs_, ...), custom_call_target="tpu_custom_call" | custom-call | bytes 50855936 | tf_op jit(solution)/shard_map/pallas_call | solution.py:1520
  423.5 1.4 fusion
  425.0 1.4 slice_reduce_fusion
  (1 shorter events, 0.0 us)
